TPU v7x, 512 devices: a whole 4x4x16 slice. The times are simulated.
512 devices in a mesh: dp: 8 (over z_lo), seq: 64 (over y, z_hi, x, core).
Axes of the slice: x: 4, y: 4, z: 16 (z_hi: 2, z_lo: 8; z = z_hi * 8 + z_lo), core: 2. Of those that a mesh axis runs over, the one named last changes fastest.
Arguments:
- activations: bfloat16 [8, 64, 512, 1024], P('dp', 'seq'), may hold values from -6 to 6
- cotangent: bfloat16 [8, 64, 512, 1024], P('dp', 'seq'), may hold values from -6 to 6
- inner_weight: bfloat16 [64, 512, 512], P('seq'), may hold values from -0.25 to 0.25
- outer_weight: bfloat16 [512, 64, 64], P('seq'), may hold values from -0.75 to 0.75
Outputs:
- input_grad: bfloat16 [8, 64, 512, 1024], P('dp', 'seq')
- inner_grad: float32 [64, 512, 512], P('seq')
- outer_grad: float32 [512, 64, 64], P('seq')
All inputs are finite; a program needn't handle non-finite values.
Results may differ from a plain program's by a relative error of at most 0.0049.
Values may be sent and summed in bfloat16 or wider, within the bound.
A program may use at most 64 MiB of HBM per device.

v0:
```python
import math

import jax
import jax.numpy as jnp
from jax import lax
from jax.sharding import PartitionSpec as P


def local(activations, cotangent, inner_weight, outer_weight):
    block = inner_weight.shape[1]
    width = activations.shape[3]
    blocks = outer_weight.shape[1]
    sequences = activations.shape[0] * lax.axis_size("dp")
    rows = lax.broadcasted_iota(jnp.int32, (block, block), 0)
    cols = lax.broadcasted_iota(jnp.int32, (block, block), 1)
    tril = (rows >= cols).astype(jnp.float32)
    brows = lax.broadcasted_iota(jnp.int32, (blocks, blocks), 0)
    bcols = lax.broadcasted_iota(jnp.int32, (blocks, blocks), 1)
    low = (brows >= bcols).astype(jnp.float32)
    inner = inner_weight * tril.astype(jnp.bfloat16)[None]
    outer = outer_weight * low.astype(jnp.bfloat16)[None]
    mixed = jnp.einsum(
        "nij,snjc->snic", inner, activations, preferred_element_type=jnp.float32
    ).astype(jnp.bfloat16)
    mixed_cols, upstream_cols = (
        lax.all_to_all(mixed, "seq", split_axis=2, concat_axis=1, tiled=True),
        lax.all_to_all(cotangent, "seq", split_axis=2, concat_axis=1, tiled=True),
    )
    outer_cols = jnp.einsum(
        "pbe,sbpc->sepc", outer, upstream_cols, preferred_element_type=jnp.float32
    ).astype(jnp.bfloat16)
    outer_sum = jnp.einsum(
        "sbpc,sepc->pbe", upstream_cols, mixed_cols, preferred_element_type=jnp.float32
    )
    mixed_grad = lax.all_to_all(outer_cols, "seq", split_axis=1, concat_axis=2, tiled=True)
    input_grad = jnp.einsum(
        "nij,snic->snjc", inner, mixed_grad, preferred_element_type=jnp.float32
    ).astype(jnp.bfloat16)
    inner_sum = jnp.einsum(
        "snic,snjc->nij", mixed_grad, activations, preferred_element_type=jnp.float32
    )
    inner_sum, outer_sum = lax.psum((inner_sum, outer_sum), "dp")
    scale = math.sqrt(sequences * width)
    inner_grad = inner_sum * tril[None] / scale
    outer_grad = outer_sum * low[None] / scale
    return (input_grad, inner_grad, outer_grad)


def solution(mesh):
    placed = (
        P("dp", "seq", None, None),
        P("dp", "seq", None, None),
        P("seq", None, None),
        P("seq", None, None),
    )
    return jax.shard_map(
        local,
        mesh=mesh,
        in_specs=placed,
        out_specs=(P("dp", "seq", None, None), P("seq", None, None), P("seq", None, None)),
        check_vma=False,
    )
```

profile of v0, /device:TPU:1, one launch (start us, length us, event | category | flops | bytes accessed | tf_op | source)
XLA Modules:
  0.0 339.3 jit_solution(13907701401318818515)
XLA Ops:
  7.2 0.0 copy-start
  7.2 2.9 copy.55
  10.1 0.5 broadcast.7
  10.6 7.8 %reduce = bf16[512,1024]{1,0:T(8,128)(2,1)} reduce(bf16[512,1,1,1024]{3,2,1,0:T(2,128)(2,1)S(1)} %bitcast.50, bf16[]{:T(256)} %broadcast.7), dimensions={1,2}, to_apply=%bitcast.47.reduce_sub_computation | reduce | bytes 2097154
  18.4 0.0 copy-start.5
  18.4 2.6 reshape.83
  21.0 22.4 %all-to-all-start = ((bf16[64,2,4096]{2,1,0:T(2,128)(2,1)}), bf16[64,2,4096]{2,1,0:T(2,128)(2,1)}, u32[]{:S(2)}, u32[]{:S(2)}) async-start(bf16[64,2,4096]{2,1,0:T(2,128)(2,1)} %reshape.83), calls=%async_computation | async-start | bytes 2097152 | tf_op jit(solution)/shard_map/all_to_all | solution.py:27
  43.4 0.0 copy-done
  43.4 0.0 copy-done.5
  43.4 0.7 fusion.2
  44.1 1.6 copy.54
  45.8 7.8 %reduce.1 = bf16[512,1024]{1,0:T(8,128)(2,1)} reduce(bf16[512,1,1,1024]{3,2,1,0:T(2,128)(2,1)S(1)} %bitcast.51, bf16[]{:T(256)} %broadcast.7), dimensions={1,2}, to_apply=%bitcast.46.reduce_sub_computation | reduce | bytes 2097154
  53.5 2.5 reshape.85
  56.0 19.0 %all-to-all-done = bf16[64,2,4096]{2,1,0:T(2,128)(2,1)} async-done(((bf16[64,2,4096]{2,1,0:T(2,128)(2,1)}), bf16[64,2,4096]{2,1,0:T(2,128)(2,1)}, u32[]{:S(2)}, u32[]{:S(2)}) %all-to-all-start) | async-done | bytes 1048608 | tf_op jit(solution)/shard_map/all_to_all | solution.py:27
  75.0 5.4 %all-to-all-start.2 = ((bf16[64,2,4096]{2,1,0:T(2,128)(2,1)}), bf16[64,2,4096]{2,1,0:T(2,128)(2,1)}, u32[]{:S(2)}, u32[]{:S(2)}) async-start(bf16[64,2,4096]{2,1,0:T(2,128)(2,1)} %reshape.85), calls=%async_computation.2 | async-start | bytes 2097152 | tf_op jit(solution)/shard_map/all_to_all | solution.py:26
  80.4 0.1 copy.29
  80.5 6.5 %reshape.84 = bf16[512,1,1,1024]{3,2,1,0:T(2,128)(2,1)S(1)} reshape(bf16[64,2,4096]{2,1,0:T(2,128)(2,1)} %all-to-all-done) | data formatting | bytes 2097152
  87.0 0.0 copy-start.4
  87.1 0.4 copy.53
  87.4 0.0 copy-start.1
  87.4 1.0 copy-done.1
  88.4 0.0 copy-done.4
  88.4 1.5 fusion
  89.9 1.6 copy.33
  91.4 19.8 %all-to-all-done.2 = bf16[64,2,4096]{2,1,0:T(2,128)(2,1)} async-done(((bf16[64,2,4096]{2,1,0:T(2,128)(2,1)}), bf16[64,2,4096]{2,1,0:T(2,128)(2,1)}, u32[]{:S(2)}, u32[]{:S(2)}) %all-to-all-start.2) | async-done | bytes 1048608 | tf_op jit(solution)/shard_map/all_to_all | solution.py:26
  111.2 14.2 %all-to-all-start.1 = ((bf16[1,64,8,1024]{3,2,0,1:T(8,128)(2,1)}), bf16[1,64,8,1024]{3,2,0,1:T(8,128)(2,1)}, u32[]{:S(2)}, u32[]{:S(2)}) async-start(bf16[1,64,8,1024]{3,2,0,1:T(8,128)(2,1)} %copy.33), calls=%async_computation.1 | async-start | bytes 2097152 | tf_op jit(solution)/shard_map/all_to_all | solution.py:35
  125.4 0.0 all-reduce.3.cloned.1.call-start
  125.5 6.5 %reshape.86 = bf16[512,1,1,1024]{3,2,1,0:T(2,128)(2,1)S(1)} reshape(bf16[64,2,4096]{2,1,0:T(2,128)(2,1)} %all-to-all-done.2) | data formatting | bytes 2097152
  132.0 0.0 copy-start.2
  132.0 0.4 copy.52
  132.4 0.8 copy-done.2
  133.2 1.9 convolution_bitcast_fusion.1
  135.1 0.0 copy-start.6
  135.1 30.9 %all-to-all-done.1 = bf16[1,64,8,1024]{3,2,0,1:T(8,128)(2,1)} async-done(((bf16[1,64,8,1024]{3,2,0,1:T(8,128)(2,1)}), bf16[1,64,8,1024]{3,2,0,1:T(8,128)(2,1)}, u32[]{:S(2)}, u32[]{:S(2)}) %all-to-all-start.1) | async-done | bytes 1048608 | tf_op jit(solution)/shard_map/all_to_all | solution.py:35
  166.1 2.9 convolution_bitcast_fusion
  169.0 0.0 all-reduce.3.cloned.1.call-update
  169.1 0.0 copy-done.6
  169.1 2.0 fusion.1
  171.0 1.3 copy.37
  172.4 156.8 %all-reduce.3.cloned.1.call-done = (f32[1,512,512]{2,1,0:T(8,128)}, f32[8,64,64]{1,2,0:T(8,128)}) async-done(((f32[1,512,512]{2,1,0:T(8,128)}, f32[8,64,64]{1,2,0:T(8,128)}), (f32[1,512,512]{2,1,0:T(8,128)}, f32[8,64,64]{1,2,0:T(8,128)})) %all-reduce.3.cloned.1.call-update) | async-done | bytes 1179664 | tf_op jit(solution)/shard_map/psum | solution.py:42
  329.2 0.0 copy-start.3
  329.2 2.4 select_multiply_fusion
  331.5 0.0 copy-done.3
  331.6 0.8 copy.38
  (3 shorter events, 0.0 us)
Async XLA Ops:
  7.2 36.2 %copy-start = (bf16[1,1,512,1024]{3,2,1,0:T(8,128)(2,1)S(1)}, bf16[1,1,512,1024]{3,2,1,0:T(8,128)(2,1)}, u32[]{:S(2)}) copy-start(bf16[1,1,512,1024]{3,2,1,0:T(8,128)(2,1)} %param.4) | copy-start | bytes 3145732
  18.4 25.0 %copy-start.5 = (bf16[1,512,512]{2,1,0:T(8,128)(2,1)S(1)}, bf16[1,512,512]{2,1,0:T(8,128)(2,1)}, u32[]{:S(2)}) copy-start(bf16[1,512,512]{2,1,0:T(8,128)(2,1)} %param.6) | copy-start | bytes 1572868
  21.0 54.1 %all-to-all-start = ((bf16[64,2,4096]{2,1,0:T(2,128)(2,1)}), bf16[64,2,4096]{2,1,0:T(2,128)(2,1)}, u32[]{:S(2)}, u32[]{:S(2)}) async-start(bf16[64,2,4096]{2,1,0:T(2,128)(2,1)} %reshape.83), calls=%async_computation | async-start | bytes 2097152 | tf_op jit(solution)/shard_map/all_to_all | solution.py:27
  75.0 36.2 %all-to-all-start.2 = ((bf16[64,2,4096]{2,1,0:T(2,128)(2,1)}), bf16[64,2,4096]{2,1,0:T(2,128)(2,1)}, u32[]{:S(2)}, u32[]{:S(2)}) async-start(bf16[64,2,4096]{2,1,0:T(2,128)(2,1)} %reshape.85), calls=%async_computation.2 | async-start | bytes 2097152 | tf_op jit(solution)/shard_map/all_to_all | solution.py:26
  87.0 1.4 copy-start.4
  87.4 1.0 copy-start.1
  111.2 54.9 %all-to-all-start.1 = ((bf16[1,64,8,1024]{3,2,0,1:T(8,128)(2,1)}), bf16[1,64,8,1024]{3,2,0,1:T(8,128)(2,1)}, u32[]{:S(2)}, u32[]{:S(2)}) async-start(bf16[1,64,8,1024]{3,2,0,1:T(8,128)(2,1)} %copy.33), calls=%async_computation.1 | async-start | bytes 2097152 | tf_op jit(solution)/shard_map/all_to_all | solution.py:35
  125.4 203.7 %all-reduce.3.cloned.1.call-start = ((), (), s32[]{:S(2)}) async-start(), calls=%async_computation.3 | async-start | bytes 2621440 | tf_op jit(solution)/shard_map/psum | solution.py:42
  132.0 1.2 copy-start.2
  135.1 33.9 %copy-start.6 = (bf16[1,512,512]{2,1,0:T(8,128)(2,1)S(1)}, bf16[1,512,512]{2,1,0:T(8,128)(2,1)}, u32[]{:S(2)}) copy-start(bf16[1,512,512]{2,1,0:T(8,128)(2,1)} %param.6) | copy-start | bytes 1572868
  329.2 2.4 copy-start.3
Sparse Core Ops, SparseCore 0:
  169.2 159.9 all-reduce.2
where the time goes:
time: 345 us; the launch traced here: 339 us
  waiting for transfers between devices  227 us (66%)
  starting transfers between devices  42.1 us (12%)
  local copies, waits for them, and re-layouts  29.5 us (9%)
  other arithmetic  17.9 us (5%)
  between operations  14.2 us (4%)
  matrix products  9 us (3%)
    psum x1, waiting for transfers between devices, local(): inner_sum, outer_sum = lax.psum((inner_sum, outer_sum), 'dp')  157 us
    all_to_all x1, waiting for transfers between devices, local(): lax.all_to_all(outer_cols, 'seq', split_axis=1, concat_axis=2, tiled=True)  30.9 us
    unnamed x24, local copies, waits for them, and re-layouts  26.3 us
    all_to_all x1, starting transfers between devices, local(): lax.all_to_all(cotangent, 'seq', split_axis=2, concat_axis=1, tiled=True)  22.4 us
    all_to_all x1, waiting for transfers between devices, local(): lax.all_to_all(mixed, 'seq', split_axis=2, concat_axis=1, tiled=True)  19.8 us
    all_to_all x1, waiting for transfers between devices, local(): lax.all_to_all(cotangent, 'seq', split_axis=2, concat_axis=1, tiled=True)  19 us
    unnamed x2, other arithmetic  15.5 us
    all_to_all x1, starting transfers between devices, local(): lax.all_to_all(outer_cols, 'seq', split_axis=1, concat_axis=2, tiled=True)  14.2 us
  transfers between devices with their start and end apart: 4, of which 4 were waited for; matrix products, arithmetic and copies ran while one was open for 10% of the time, Pallas kernels for 0%

commit v1 on v0

v1 whole, which is shorter than its diff:
```python
import functools
import math

import jax
import jax.numpy as jnp
from jax import lax
from jax.experimental import pallas as pl
from jax.experimental.pallas import tpu as pltpu
from jax.sharding import PartitionSpec as P

MESH = pl.DeviceIdType.MESH
BF = jnp.bfloat16
F32 = jnp.float32

B = 512
D = 1024
NC = 4
CW = D // NC
PD = 32
PP = 16
NZ = 16
OFFS = (0, 128, 384, 768)
PACK = 1280


def coords():
    lo = lax.axis_index("dp")
    s = lax.axis_index("seq")
    core = lax.rem(s, 2)
    x = lax.rem(s // 2, 4)
    h = lax.rem(s // 8, 2)
    y = s // 16
    return lo, y, h, x, core


def plane_peer(i):
    lo, y, h, x, core = coords()
    px = lax.rem(x + lax.rem(i // 2, 4), 4)
    py = lax.rem(y + i // 8, 4)
    pc = lax.rem(core + i, 2)
    return py * 8 + px * 2 + pc, (lo, py * 16 + h * 8 + px * 2 + pc)


def ring_peer(i):
    lo, y, h, x, core = coords()
    z = lax.rem(h * 8 + lo + i, NZ)
    return z, (lax.rem(z, 8), y * 16 + (z // 8) * 8 + x * 2 + core)


def dp_peer(i):
    lo, y, h, x, core = coords()
    t = lax.rem(lo + i, 8)
    return t, (t, y * 16 + h * 8 + x * 2 + core)


def remote(src, dst, send, recv, device):
    return pltpu.make_async_remote_copy(
        src_ref=src, dst_ref=dst, send_sem=send, recv_sem=recv, device_id=device, device_id_type=MESH
    )


def wait_bytes(ref, sem):
    pltpu.make_async_copy(ref, ref, sem).wait()


def iota(shape, dim):
    return lax.broadcasted_iota(jnp.int32, shape, dim)


def dot_nt(a, b):
    return lax.dot_general(a, b, (((1,), (1,)), ((), ())), preferred_element_type=F32)


def dot_nn(a, b):
    return lax.dot_general(a, b, (((1,), (0,)), ((), ())), preferred_element_type=F32)


def dot_tn(a, b):
    return lax.dot_general(a, b, (((0,), (0,)), ((), ())), preferred_element_type=F32)


def halves(a, b):
    first = jnp.concatenate([a[:8], b[:8]], axis=0)
    second = jnp.concatenate([a[8:], b[8:]], axis=0)
    return first.astype(BF), second.astype(BF)


def kernel(
    act, cot, inner, outer, ig_out, inner_out, outer_out,
    cot_s, blk, x_s, x_r, g_s, g_r, inner_p, inner_t, ow, tmat, wmat, s_acc, i_acc,
    rs_s, rs_r, ag, ss_s, ss_r, sg,
    c_ss, c_rs, z_ss, z_rs, x_ss, x_rs, g_ss, g_rs, o_sem, rs_sem, ag_sem, ss_sem, sg_sem,
):
    lo, y, h, x, core = coords()
    me = y * 8 + x * 2 + core
    zme = h * 8 + lo
    scale = 1.0 / math.sqrt(8192.0)

    barrier = pltpu.get_barrier_semaphore()

    @pl.loop(1, PD)
    def _(i):
        pl.semaphore_signal(barrier, inc=1, device_id=plane_peer(i)[1], device_id_type=MESH)

    @pl.loop(1, NZ)
    def _(i):
        pl.semaphore_signal(barrier, inc=1, device_id=ring_peer(i)[1], device_id_type=MESH)

    @pl.loop(0, 16)
    def _(q):
        big, u = q // 4, lax.rem(q, 4)
        at = pl.multiple_of(big * 128 + u * 16, 16)
        a = cot[pl.ds(at, 16), :].astype(F32)
        b = cot[pl.ds(at + 64, 16), :].astype(F32)
        first, second = halves(a, b)
        for k in range(NC):
            cot_s[k, big * 8 + u * 2] = first[:, k * CW:(k + 1) * CW]
            cot_s[k, big * 8 + u * 2 + 1] = second[:, k * CW:(k + 1) * CW]

    pl.semaphore_wait(barrier, PD - 1 + NZ - 1)

    def a2a_start(src, dst, send, recv):
        @pl.loop(1, PD)
        def _(i):
            d, device = plane_peer(i)
            remote(src(d), dst(me), send, recv, device).start()

        pltpu.make_async_copy(src(me), dst(me), recv).start()

    mine = h * PD
    for k in range(NC):
        a2a_start(lambda d: cot_s.at[k, d], lambda d: blk.at[k, mine + d], c_ss.at[k], c_rs.at[k])
        if k == 0:
            pltpu.make_async_copy(outer, ow.at[h], o_sem.at[2]).start()
            remote(outer, ow.at[h], o_sem.at[0], o_sem.at[1], ring_peer(8)[1]).start()

    def cross(k, part):
        rows = pl.ds(mine + part * 8, 8)
        return remote(blk.at[k, rows], blk.at[k, rows], z_ss.at[k, part], z_rs.at[k, part], ring_peer(8)[1])

    for k in range(NC):
        wait_bytes(blk.at[k, pl.ds(mine, PD)], c_rs.at[k])
        for part in range(4):
            cross(k, part).start()

    @pl.loop(0, 16)
    def _(q):
        big, u = q // 4, lax.rem(q, 4)
        at = pl.multiple_of(big * 128 + u * 16, 16)

        def rows(start):
            v = inner[pl.ds(start, 16), :].astype(F32)
            return jnp.where(iota((16, B), 0) + start >= iota((16, B), 1), v, 0.0)

        first, second = halves(rows(at), rows(at + 64))
        to = pl.multiple_of(big * 128 + u * 32, 32)
        inner_p[pl.ds(to, 16), :] = first
        inner_p[pl.ds(to + 16, 16), :] = second

    inner_t[...] = inner_p[...].T

    @pl.loop(0, 4)
    def _(q):
        rows = pl.ds(pl.multiple_of(q * 128, 128), 128)
        v = dot_nn(inner_p[rows, :], act[...]).astype(BF)
        x_s[pl.ds(q * 8, 8)] = v.reshape(8, PP, D)

    a2a_start(lambda d: x_s.at[d], lambda d: x_r.at[d], x_ss, x_rs)

    pltpu.make_async_copy(outer, ow.at[h], o_sem.at[2]).wait()
    wait_bytes(ow.at[1 - h], o_sem.at[1])
    pick = (iota((32, 64), 1) == 16 * (iota((32, 64), 0) // 8) + 8 * h + lax.rem(iota((32, 64), 0), 8)).astype(BF)
    low = (iota((64, 64), 0) >= iota((64, 64), 1)).astype(F32)
    for hh in range(2):
        @pl.loop(0, 8)
        def _(t):
            v = (ow[hh, t].astype(F32) * low).astype(BF)
            tmat[hh * 8 + t] = dot_nt(pick, v).astype(BF)

    n_r = iota((128, 512), 0)
    n_c = iota((128, 512), 1)
    e_r = iota((64, 1024), 0)
    e_c = iota((64, 1024), 1) // 16
    bl = lax.rem(e_c, 32)
    spread = (e_r == 16 * (bl // 8) + 8 * (e_c // 32) + lax.rem(bl, 8)).astype(BF)

    @pl.loop(0, 4)
    def _(q):
        row = n_r + q * 128
        perm = (n_c == lax.rem(row, 16) * 32 + row // 16).astype(BF)
        t2 = dot_nn(perm, tmat[...].reshape(512, 64)).astype(BF)
        w = dot_nn(t2, spread)
        same = lax.rem(iota((128, 1024), 0), 16) == lax.rem(iota((128, 1024), 1), 16)
        wmat[pl.ds(pl.multiple_of(q * 128, 128), 128), :] = jnp.where(same, w, 0.0).astype(BF)

    def mix(k):
        wait_other = pl.ds((1 - h) * PD, PD)
        for part in range(4):
            rows = pl.ds((1 - h) * PD + part * 8, 8)
            wait_bytes(blk.at[k, rows], z_rs.at[k, part])

        @pl.loop(0, 4)
        def _(q):
            rows = pl.ds(pl.multiple_of(q * 128, 128), 128)
            v = dot_nn(wmat[rows, :], blk[k].reshape(1024, CW)).astype(BF)
            g_s[k, pl.ds(q * 8, 8)] = v.reshape(8, PP, CW)

        a2a_start(lambda d: g_s.at[k, d], lambda d: g_r.at[k, d], g_ss.at[k], g_rs.at[k])

    def outer_part(k):
        if k == 0:
            wait_bytes(x_r, x_rs)

        @pl.loop(0, 8)
        def _(q):
            rows = pl.ds(pl.multiple_of(q * 128, 128), 128)
            v = dot_nt(blk[k, pl.ds(q * 8, 8)].reshape(128, CW), x_r[:, :, k * CW:(k + 1) * CW].reshape(512, CW))
            if k == 0:
                s_acc[rows, :] = v
            else:
                s_acc[rows, :] += v

    def back(k):
        wait_bytes(g_r.at[k], g_rs.at[k])
        cols = slice(k * CW, (k + 1) * CW)

        @pl.loop(0, 4)
        def _(q):
            rows = pl.ds(pl.multiple_of(q * 128, 128), 128)
            v = dot_nt(g_r[k, pl.ds(q * 8, 8)].reshape(128, CW), act[:, cols])
            if k == 0:
                i_acc[rows, :] = v
            else:
                i_acc[rows, :] += v

    def back_input(k):
        cols = slice(k * CW, (k + 1) * CW)

        @pl.loop(0, 4)
        def _(q):
            rows = pl.ds(pl.multiple_of(q * 128, 128), 128)
            ig_out[rows, cols] = dot_nn(inner_t[rows, :], g_r[k].reshape(512, CW)).astype(BF)

    inner_out[...] = jnp.zeros_like(inner_out)

    for k in range(NC):
        mix(k)
        outer_part(k)
        if k > 0:
            back(k - 1)
            back_input(k - 1)

    packed = jnp.zeros((256, 128), F32)
    same = lax.rem(iota((256, 512), 0), 16) == lax.rem(iota((256, 512), 1), 16)
    for bh in range(4):
        v = jnp.where(same, s_acc[bh * 256:(bh + 1) * 256, :], 0.0).astype(BF)
        put = (iota((512, 128), 1) == 32 * bh + iota((512, 128), 0) // 16).astype(BF)
        packed = packed + dot_nn(v, put)
    ss_s[...] = packed.astype(BF).reshape(8, 32, 128)

    def scatter(src, dst, sem):
        @pl.loop(1, 8)
        def _(i):
            t, device = dp_peer(i)
            remote(src.at[t], dst.at[lo], sem.at[0], sem.at[1], device).start()

        pltpu.make_async_copy(src.at[lo], dst.at[lo], sem.at[1]).start()

    scatter(ss_s, ss_r, ss_sem)

    back(NC - 1)
    for big in range(4):
        w = 128 * (big + 1)
        v = i_acc[big * 128:(big + 1) * 128, :w].astype(BF)
        rs_s[:, :, OFFS[big]:OFFS[big] + w] = v.reshape(8, 16, w)
    scatter(rs_s, rs_r, rs_sem)
    back_input(NC - 1)

    wait_bytes(ss_r, ss_sem.at[1])
    total = ss_r[0].astype(F32)
    for i in range(1, 8):
        total = total + ss_r[i].astype(F32)
    sg[zme] = total.astype(BF)

    @pl.loop(1, NZ)
    def _(i):
        remote(sg.at[zme], sg.at[zme], sg_sem.at[0], sg_sem.at[1], ring_peer(i)[1]).start()

    wait_bytes(rs_r, rs_sem.at[1])
    total = rs_r[0].astype(F32)
    for i in range(1, 8):
        total = total + rs_r[i].astype(F32)
    ag[lo] = total.astype(BF)

    @pl.loop(1, 8)
    def _(i):
        remote(ag.at[lo], ag.at[lo], ag_sem.at[0], ag_sem.at[1], dp_peer(i)[1]).start()

    wait_bytes(sg.at[pl.ds(0, NZ - 1)], sg_sem.at[1])
    parts = []
    for hs in range(2):
        v = sg[hs * 8:(hs + 1) * 8].astype(F32).reshape(16, 16, 128)
        v = jnp.where(h == 0, v[:, :8], v[:, 8:])
        parts.append(v.reshape(128, 128).astype(BF))
    c_r = iota((128, 64), 0)
    c_c = iota((128, 64), 1)
    for bh in range(4):
        v = jnp.zeros((128, 64), F32)
        for hs in range(2):
            el = c_r - 32 * bh
            col = (el >= 0) & (el < 32) & (c_c == 16 * (el // 8) + 8 * hs + lax.rem(el, 8))
            v = v + dot_nn(parts[hs], col.astype(BF))
        for g in range(2):
            base = 32 * (bh % 2) + 16 * g + 8 * (bh // 2)
            keep = iota((8, 8, 64), 0) + base >= iota((8, 8, 64), 2)
            outer_out[base:base + 8] = jnp.where(keep, v[64 * g:64 * g + 64].reshape(8, 8, 64) * scale, 0.0)

    wait_bytes(ag.at[pl.ds(0, 7)], ag_sem.at[1])
    for big in range(4):
        w = 128 * (big + 1)
        v = ag[:, :, OFFS[big]:OFFS[big] + w].astype(F32)
        for hh in range(2):
            start = big * 128 + hh * 64
            part = v[:, 8 * hh:8 * hh + 8, :].reshape(64, w) * scale
            keep = iota((64, w), 0) + start >= iota((64, w), 1)
            inner_out[start:start + 64, :w] = jnp.where(keep, part, 0.0)

    for k in range(NC):
        wait_bytes(cot_s.at[k, pl.ds(0, PD - 1)], c_ss.at[k])
        wait_bytes(g_s.at[k, pl.ds(0, PD - 1)], g_ss.at[k])
        for part in range(4):
            cross(k, part).wait_send()
    wait_bytes(x_s.at[pl.ds(0, PD - 1)], x_ss)
    wait_bytes(outer, o_sem.at[0])
    wait_bytes(ss_s.at[pl.ds(0, 7)], ss_sem.at[0])
    wait_bytes(rs_s.at[pl.ds(0, 7)], rs_sem.at[0])
    wait_bytes(ag.at[pl.ds(0, 7)], ag_sem.at[0])
    wait_bytes(sg.at[pl.ds(0, NZ - 1)], sg_sem.at[0])


def local(activations, cotangent, inner_weight, outer_weight):
    vmem = pl.BlockSpec(memory_space=pltpu.VMEM)
    dma = pltpu.SemaphoreType.DMA
    scratch = [
        pltpu.VMEM((NC, PD, PP, CW), BF),
        pltpu.VMEM((NC, 2 * PD, PP, CW), BF),
        pltpu.VMEM((PD, PP, D), BF),
        pltpu.VMEM((PD, PP, D), BF),
        pltpu.VMEM((NC, PD, PP, CW), BF),
        pltpu.VMEM((NC, PD, PP, CW), BF),
        pltpu.VMEM((B, B), BF),
        pltpu.VMEM((B, B), BF),
        pltpu.VMEM((2, 8, 64, 64), BF),
        pltpu.VMEM((16, 32, 64), BF),
        pltpu.VMEM((512, 1024), BF),
        pltpu.VMEM((1024, 512), F32),
        pltpu.VMEM((B, B), F32),
        pltpu.VMEM((8, 16, PACK), BF),
        pltpu.VMEM((8, 16, PACK), BF),
        pltpu.VMEM((8, 16, PACK), BF),
        pltpu.VMEM((8, 32, 128), BF),
        pltpu.VMEM((8, 32, 128), BF),
        pltpu.VMEM((NZ, 32, 128), BF),
        dma((NC,)), dma((NC,)),
        dma((NC, 4)), dma((NC, 4)),
        dma, dma,
        dma((NC,)), dma((NC,)),
        dma((3,)), dma((2,)), dma((2,)), dma((2,)), dma((2,)),
    ]
    ig, inner_grad, outer_grad = pl.pallas_call(
        kernel,
        out_shape=(
            jax.ShapeDtypeStruct((B, D), BF),
            jax.ShapeDtypeStruct((B, B), F32),
            jax.ShapeDtypeStruct((64, 8, 64), F32),
        ),
        in_specs=[vmem] * 4,
        out_specs=(vmem, vmem, vmem),
        scratch_shapes=scratch,
        compiler_params=pltpu.CompilerParams(
            collective_id=0, has_side_effects=True, vmem_limit_bytes=48 * 1024 * 1024
        ),
        cost_estimate=pl.CostEstimate(flops=8_000_000_000, bytes_accessed=6_000_000, transcendentals=0),
        name="mixer",
    )(activations[0, 0], cotangent[0, 0], inner_weight[0], outer_weight)
    return ig[None, None], inner_grad[None], jnp.transpose(outer_grad, (1, 0, 2))


def solution(mesh):
    placed = (
        P("dp", "seq", None, None),
        P("dp", "seq", None, None),
        P("seq", None, None),
        P("seq", None, None),
    )
    return jax.shard_map(
        local,
        mesh=mesh,
        in_specs=placed,
        out_specs=(P("dp", "seq", None, None), P("seq", None, None), P("seq", None, None)),
        check_vma=False,
    )
```

time: 345 us -> 173 us (0.50)
  waiting for transfers between devices: 227 us -> 0 us
  Pallas kernels: 0 us -> 162 us
  starting transfers between devices: 42.1 us -> 0 us
  local copies, waits for them, and re-layouts: 29.5 us -> 7.08 us
  other arithmetic: 17.9 us -> 0 us
  between operations: 14.2 us -> 0.65 us
  matrix products: 9 us -> 0 us
    pallas_call x0 -> x1, Pallas kernels: none -> 162 us  [local(): pl.pallas_call(kernel, out_shape=(jax.ShapeDtypeStruct((B, D), BF), jax.S...]
    psum x1 -> x0, waiting for transfers between devices: 157 us -> none  [local(): inner_sum, outer_sum = lax.psum((inner_sum, outer_sum), 'dp')]
    all_to_all x3 -> x0, waiting for transfers between devices: 69.7 us -> none  [the longest x1 30.9 us: local(): lax.all_to_all(outer_cols, 'seq', split_axis=1, concat_axis=2, tiled=True)]
    all_to_all x3 -> x0, starting transfers between devices: 42 us -> none  [the longest x1 22.4 us: local(): lax.all_to_all(cotangent, 'seq', split_axis=2, concat_axis=1, tiled=True)]
    unnamed x24 -> x11, local copies, waits for them, and re-layouts: 26.3 us -> 7.08 us
    unnamed x2 -> x0, other arithmetic: 15.5 us -> none
    dot_general x5 -> x0, matrix products: 9 us -> none  [the longest x1 2.94 us: local(): jnp.einsum('snic,snjc->nij', mixed_grad, activations, preferred_element_t...]
  transfers between devices with their start and end apart: 4 -> 0, of which waited for: 4 -> 0; matrix products, arithmetic and copies ran while one was open for 10% -> 0% of each run, Pallas kernels for 0% -> 0%
where the time goes in v1:
time: 173 us; the launch traced here: 170 us
  Pallas kernels  162 us (94%)
  local copies, waits for them, and re-layouts  7.08 us (4%)
    pallas_call x1, Pallas kernels, local(): pl.pallas_call(kernel, out_shape=(jax.ShapeDtypeStruct((B, D), BF), jax.S...  162 us
    unnamed x11, local copies, waits for them, and re-layouts  7.08 us

profile of v1, /device:TPU:1, one launch (start us, length us, event | category | flops | bytes accessed | tf_op | source)
XLA Modules:
  0.0 169.5 jit_solution(8259940111880369406)
XLA Ops:
  0.6 0.0 copy-start
  0.6 1.2 copy-done
  1.9 0.0 copy-start.1
  1.9 1.2 copy-done.1
  3.1 0.0 copy-start.2
  3.1 1.0 copy-done.2
  4.1 0.0 copy-start.3
  4.1 0.9 copy-done.3
  5.0 161.8 %mixer.1 = (bf16[512,1024]{1,0:T(8,128)(2,1)S(1)}, f32[512,512]{1,0:T(8,128)S(1)}, f32[64,8,64]{2,1,0:T(8,128)S(1)}) custom-call(bf16[512,1024]{1,0:T(8,128)(2,1)S(1)} %bitcast.9, bf16[512,1024]{1,0:T(8,128)(2,1)S(1)} %bitcast.10, bf16[512,512]{1,0:T(8,128)(2,1)S(1)} %bitcast.11, bf16[8,64,64]{2,1,0:T(8,128)(2,1)S(1)} %copy-done.3), custom_call_target="tpu_custom_call" | custom-call | flops 8000000000 | bytes 6000000 | tf_op jit(solution)/shard_map/mixer/pallas_call | solution.py:370
  166.8 0.8 copy.7
  167.6 1.0 copy.10
  168.6 1.0 copy.11
Async XLA Ops:
  0.6 1.2 copy-start
  1.9 1.2 copy-start.1
  3.1 1.0 copy-start.2
  4.1 0.9 copy-start.3

commit v2 on v0

v2 whole, which is shorter than its diff:
```python
import functools
import math

import jax
import jax.numpy as jnp
from jax import lax
from jax.experimental import pallas as pl
from jax.experimental.pallas import tpu as pltpu
from jax.sharding import PartitionSpec as P

MESH = pl.DeviceIdType.MESH
BF = jnp.bfloat16
F32 = jnp.float32

B = 512
D = 1024
NI = 4
CW = D // NI
PD = 32
PP = 16
NZ = 16
OFFS = (0, 128, 384, 768)
ORDER = (3, 2, 1, 0)
PARTS = 4
PACK = 1280


def coords():
    lo = lax.axis_index("dp")
    s = lax.axis_index("seq")
    core = lax.rem(s, 2)
    x = lax.rem(s // 2, 4)
    h = lax.rem(s // 8, 2)
    y = s // 16
    return lo, y, h, x, core


def plane_peers():
    lo, y, h, x, core = coords()
    offs = []
    for b in range(4):
        for c in range(2):
            offs.append(lax.rem(x + b, 4) * 2 + lax.rem(core + c, 2))

    def row(a):
        py = lax.rem(y + a, 4)
        return py * 8, py * 16 + h * 8

    return row, offs, lo


def ring_peer(i):
    lo, y, h, x, core = coords()
    z = lax.rem(h * 8 + lo + i, NZ)
    return z, (lax.rem(z, 8), y * 16 + (z // 8) * 8 + x * 2 + core)


def dp_peer(i):
    lo, y, h, x, core = coords()
    t = lax.rem(lo + i, 8)
    return t, (t, y * 16 + h * 8 + x * 2 + core)


def remote(src, dst, send, recv, device):
    return pltpu.make_async_remote_copy(
        src_ref=src, dst_ref=dst, send_sem=send, recv_sem=recv, device_id=device, device_id_type=MESH
    )


def wait_bytes(ref, sem):
    pltpu.make_async_copy(ref, ref, sem).wait()


def iota(shape, dim):
    return lax.broadcasted_iota(jnp.int32, shape, dim)


def dot_nt(a, b):
    return lax.dot_general(a, b, (((1,), (1,)), ((), ())), preferred_element_type=F32)


def dot_nn(a, b):
    return lax.dot_general(a, b, (((1,), (0,)), ((), ())), preferred_element_type=F32)


def dot_tn(a, b):
    return lax.dot_general(a, b, (((0,), (0,)), ((), ())), preferred_element_type=F32)


def halves(a, b):
    first = jnp.concatenate([a[:8], b[:8]], axis=0)
    second = jnp.concatenate([a[8:], b[8:]], axis=0)
    return first.astype(BF), second.astype(BF)


def kernel(
    act_in, cot_in, inner_in, outer_in, ig_res, ag_res, sg_res,
    act, cot, inner, outer, cot_s, blk, g_s, g_r, x_s, x_r, inner_p, inner_t,
    oscr, ot, ow, wmat, ig_out, ig_acc, rs_s, rs_r, ag, sy_s, sy_r, ss_s, ss_r, sg,
    in_sem, c_ss, c_rs, z_ss, z_rs, x_sem, g_ss, g_rs, o_ss, o_rs, rs_ss, rs_rs, ag_ss, ag_rs,
    sy_ss, sy_rs, ss_sem, sg_sem, out_sem,
):
    lo, y, h, x, core = coords()
    me = y * 8 + x * 2 + core
    zme = h * 8 + lo
    peer_row, peer_offs, _ = plane_peers()
    mine = h * PD
    other = (1 - h) * PD

    def column_peer(a):
        py = lax.rem(y + a, 4)
        return py, (lo, py * 16 + h * 8 + x * 2 + core)

    loads = [
        pltpu.make_async_copy(a, b, in_sem.at[n])
        for n, (a, b) in enumerate(((cot_in, cot), (outer_in, outer), (inner_in, inner), (act_in, act)))
    ]
    for load in loads:
        load.start()

    barrier = pltpu.get_barrier_semaphore()

    @pl.loop(1, NZ)
    def _(i):
        pl.semaphore_signal(barrier, inc=1, device_id=ring_peer(i)[1], device_id_type=MESH)

    def plane_loop(body):
        @pl.loop(0, 4)
        def _(a):
            place, seq = peer_row(a)
            for off in peer_offs[1:]:
                body(place + off, (lo, seq + off))

        @pl.loop(1, 4)
        def _(a):
            place, seq = peer_row(a)
            body(place + peer_offs[0], (lo, seq + peer_offs[0]))

    plane_loop(lambda d, device: pl.semaphore_signal(barrier, inc=1, device_id=device, device_id_type=MESH))

    loads[0].wait()

    @pl.loop(0, 16)
    def _(q):
        big, u = q // 4, lax.rem(q, 4)
        at = pl.multiple_of(big * 128 + u * 16, 16)
        a = cot[pl.ds(at, 16), :].astype(F32)
        b = cot[pl.ds(at + 64, 16), :].astype(F32)
        first, second = halves(a, b)
        for quarter in range(4):
            cols = slice(quarter * CW, (quarter + 1) * CW)
            cot_s[big, quarter * 8 + u * 2] = first[:, cols]
            cot_s[big, quarter * 8 + u * 2 + 1] = second[:, cols]

    loads[1].wait()
    low = iota((64, 64), 0) >= iota((64, 64), 1)
    for t in range(8):
        v = jnp.where(low, outer[t].astype(F32), 0.0)
        oscr[pl.ds(t, 32, stride=8), :] = jnp.concatenate([v[:32], v[32:]], axis=1)
    ot[...] = oscr[...].astype(BF)

    pl.semaphore_wait(barrier, PD - 1 + NZ - 1)

    def a2a_start(src, dst, send, recv):
        plane_loop(lambda d, device: remote(src(d), dst(me), send, recv, device).start())
        pltpu.make_async_copy(src(me), dst(me), recv).start()

    def cross(t, part):
        size = PD // PARTS
        rows = blk.at[ORDER[t], pl.ds(mine + part * size, size)]
        return remote(rows, rows, z_ss.at[t, part], z_rs.at[t, part], ring_peer(8)[1])

    def cross_start(t):
        @pl.when(h == 1)
        def _():
            cross(t, 0).start()

        for part in range(1, PARTS):
            cross(t, part).start()

    def cross_wait(t):
        size = PD // PARTS
        @pl.when(h == 0)
        def _():
            wait_bytes(blk.at[ORDER[t], pl.ds(other, size)], z_rs.at[t, 0])

        for part in range(1, PARTS):
            wait_bytes(blk.at[ORDER[t], pl.ds(other + part * size, size)], z_rs.at[t, part])

    def own_start(t):
        k = ORDER[t]
        a2a_start(lambda d: cot_s.at[k, d], lambda d: blk.at[k, mine + d], c_ss.at[t], c_rs.at[t])

    def own_wait(t):
        wait_bytes(blk.at[ORDER[t], pl.ds(mine, PD)], c_rs.at[t])

    for t in range(NI):
        own_start(t)
        if t == 0:
            for a in range(1, 4):
                remote(ot, ow.at[y, h], o_ss.at[a], o_rs.at[a], column_peer(a)[1]).start()
            remote(ot, ow.at[y, h], o_ss.at[0], o_rs.at[0], ring_peer(8)[1]).start()
            own_copy = pltpu.make_async_copy(ot, ow.at[y, h], o_rs.at[7])
            own_copy.start()
        if t > 0:
            own_wait(t - 1)
            cross_start(t - 1)
    own_wait(NI - 1)
    cross_start(NI - 1)

    loads[2].wait()

    @pl.loop(0, 16)
    def _(q):
        big, u = q // 4, lax.rem(q, 4)
        at = pl.multiple_of(big * 128 + u * 16, 16)

        def rows(start):
            v = inner[pl.ds(start, 16), :].astype(F32)
            return jnp.where(iota((16, B), 0) + start >= iota((16, B), 1), v, 0.0)

        first, second = halves(rows(at), rows(at + 64))
        to = pl.multiple_of(big * 128 + u * 32, 32)
        inner_p[pl.ds(to, 16), :] = first
        inner_p[pl.ds(to + 16, 16), :] = second

    inner_t[...] = inner_p[...].T
    loads[3].wait()

    @pl.loop(0, 4)
    def _(q):
        rows = pl.ds(pl.multiple_of(q * 128, 128), 128)
        v = dot_nn(inner_p[rows, :], act[...]).astype(BF)
        for quarter in range(4):
            cols = slice(quarter * CW, (quarter + 1) * CW)
            x_s[quarter * 8:(quarter + 1) * 8, q] = v[:, cols].reshape(8, PP, CW)

    a2a_start(lambda d: x_s.at[d], lambda d: x_r.at[d], x_sem.at[0], x_sem.at[1])

    def outer_pass():
        wait_bytes(ow.at[y, 1 - h], o_rs.at[0])
        for a in range(1, 4):
            remote(ow.at[y, 1 - h], ow.at[y, 1 - h], o_ss.at[3 + a], o_rs.at[3 + a], column_peer(a)[1]).start()

    def outer_wait():
        own_copy.wait()
        for a in range(1, 4):
            src = lax.rem(y + 4 - a, 4)
            wait_bytes(ow.at[src, h], o_rs.at[a])
            wait_bytes(ow.at[src, 1 - h], o_rs.at[3 + a])

    def build(k):
        el = iota((64, 512), 1) // 16
        pick = (iota((64, 512), 0) == 16 * (el // 8) + 8 * h + lax.rem(el, 8)).astype(BF)
        same = lax.rem(iota((128, 512), 0), 16) == lax.rem(iota((128, 512), 1), 16)

        @pl.loop(0, 8)
        def _(g):
            group = 2 * lax.rem(g, 4) + g // 4
            rows = pl.ds(pl.multiple_of(lax.rem(group, 4) * 64, 64), 64)
            both = []
            for hh in range(2):
                v = ow[k, hh, rows, :].astype(F32)
                both.append(jnp.where(group < 4, v[:, :64], v[:, 64:]).reshape(8, 8, 64))
            v = jnp.concatenate(both, axis=1).reshape(128, 64).astype(BF)
            w = jnp.where(same, dot_nn(v, pick), 0.0).astype(BF)
            wmat[k, :, pl.ds(pl.multiple_of(g * 128, 128), 128)] = w.T

    def mix(t):
        k = ORDER[t]
        cross_wait(t)

        @pl.loop(0, 4)
        def _(a):
            place, seq = peer_row(a)
            rows = pl.ds(pl.multiple_of(place * PP, 128), 128)
            v = dot_nn(wmat[k, rows, :], blk[k].reshape(1024, CW)).astype(BF)
            g_s[k, pl.ds(place, 8)] = v.reshape(8, PP, CW)

            def give(off):
                remote(
                    g_s.at[k, place + off], g_r.at[k, me], g_ss.at[t], g_rs.at[t], (lo, seq + off)
                ).start()

            for off in peer_offs[1:]:
                give(off)

            @pl.when(a > 0)
            def _():
                give(peer_offs[0])

        pltpu.make_async_copy(g_s.at[k, me], g_r.at[k, me], g_rs.at[t]).start()

    def outer_part(t):
        k = ORDER[t]
        if t == 0:
            wait_bytes(x_r, x_sem.at[1])
        same = lax.rem(iota((128, 512), 0), 16) == lax.rem(iota((128, 512), 1), 16)

        @pl.loop(0, 2)
        def _(half):
            total = jnp.zeros((128, 128), F32)
            for bh in range(4):
                v = dot_nt(blk[k, pl.ds(bh * 16 + half * 8, 8)].reshape(128, CW), x_r[:, k].reshape(512, CW))
                put = (iota((512, 128), 1) == 32 * bh + iota((512, 128), 0) // 16).astype(BF)
                total = total + dot_nn(jnp.where(same, v, 0.0).astype(BF), put)
            sy_s[k, pl.ds(pl.multiple_of(half * 128, 128), 128), :] = total.astype(BF)

        @pl.when(y == k)
        def _():
            pltpu.make_async_copy(sy_s.at[k], sy_r.at[y], sy_rs.at[y]).start()

        @pl.when(y != k)
        def _():
            device = (lo, k * 16 + h * 8 + x * 2 + core)
            remote(sy_s.at[k], sy_r.at[y], sy_ss.at[k], sy_rs.at[y], device).start()

    def back(t):
        k = ORDER[t]
        w = 128 * (k + 1)
        wait_bytes(g_r.at[k], g_rs.at[t])
        v = jnp.zeros((128, w), F32)
        for quarter in range(4):
            cols = slice(quarter * CW, (quarter + 1) * CW)
            v = v + dot_nt(g_r[k, quarter * 8:(quarter + 1) * 8].reshape(128, CW), act[:w, cols])
        cols = slice(OFFS[k], OFFS[k] + w)
        rs_s[:, :, cols] = v.astype(BF).reshape(8, 16, w)

        @pl.loop(1, 8)
        def _(i):
            to, device = dp_peer(i)
            remote(rs_s.at[to, :, cols], rs_r.at[lo, :, cols], rs_ss.at[t], rs_rs.at[t], device).start()

        pltpu.make_async_copy(rs_s.at[lo, :, cols], rs_r.at[lo, :, cols], rs_rs.at[t]).start()

    def back_input(t):
        k = ORDER[t]
        w = 128 * (k + 1)
        for quarter in range(4):
            cols = slice(quarter * CW, (quarter + 1) * CW)
            g = g_r[k, quarter * 8:(quarter + 1) * 8].reshape(128, CW)
            v = dot_nn(inner_t[:w, k * 128:(k + 1) * 128], g)
            if t > 0:
                v = v + ig_acc[:w, cols]
            ig_out[k * 128:w, cols] = v[k * 128:].astype(BF)
            if k > 0:
                ig_acc[:k * 128, cols] = v[:k * 128]
        ig_copy(t).start()

    def gather(t):
        k = ORDER[t]
        w = 128 * (k + 1)
        cols = slice(OFFS[k], OFFS[k] + w)
        wait_bytes(rs_r.at[:, :, cols], rs_rs.at[t])
        total = rs_r[0, :, cols].astype(F32)
        for i in range(1, 8):
            total = total + rs_r[i, :, cols].astype(F32)
        ag[lo, :, cols] = total.astype(BF)

        @pl.loop(1, 8)
        def _(i):
            remote(ag.at[lo, :, cols], ag.at[lo, :, cols], ag_ss.at[t], ag_rs.at[t], dp_peer(i)[1]).start()

    def ig_copy(t):
        rows = pl.ds(ORDER[t] * 128, 128)
        return pltpu.make_async_copy(ig_out.at[rows], ig_res.at[rows], out_sem.at[t])

    def ag_copy(t):
        cols = slice(OFFS[ORDER[t]], OFFS[ORDER[t]] + 128 * (ORDER[t] + 1))
        return pltpu.make_async_copy(ag.at[:, :, cols], ag_res.at[:, :, cols], out_sem.at[NI + t])

    def inner_result(t):
        cols = slice(OFFS[ORDER[t]], OFFS[ORDER[t]] + 128 * (ORDER[t] + 1))
        wait_bytes(ag.at[pl.ds(0, 7), :, cols], ag_rs.at[t])
        ag_copy(t).start()

    @pl.when(h == 1)
    def _():
        blk[:, :8] = jnp.zeros((NI, 8, PP, CW), BF)


    outer_pass()
    outer_wait()
    for t in range(NI):
        build(ORDER[t])
    for t in range(NI - 1):
        mix(t)
        outer_part(t)
        back(t)
        back_input(t)
        if t == 2:
            gather(0)

    mix(3)
    outer_part(3)
    back(3)

    for a in range(4):
        src = lax.rem(y + a, 4)
        wait_bytes(sy_r.at[src], sy_rs.at[src])
    v = sy_r[0].astype(F32) + sy_r[1].astype(F32) + sy_r[2].astype(F32) + sy_r[3].astype(F32)
    ss_s[...] = v.astype(BF).reshape(8, 32, 128)

    @pl.loop(1, 8)
    def _(i):
        to, device = dp_peer(i)
        remote(ss_s.at[to], ss_r.at[lo], ss_sem.at[0], ss_sem.at[1], device).start()

    pltpu.make_async_copy(ss_s.at[lo], ss_r.at[lo], ss_sem.at[1]).start()

    gather(1)
    gather(2)
    back_input(3)
    inner_result(0)
    gather(3)

    wait_bytes(ss_r, ss_sem.at[1])
    total = ss_r[0].astype(F32)
    for i in range(1, 8):
        total = total + ss_r[i].astype(F32)
    sg[zme] = total.astype(BF)

    @pl.loop(1, NZ)
    def _(i):
        remote(sg.at[zme], sg.at[zme], sg_sem.at[0], sg_sem.at[1], ring_peer(i)[1]).start()

    inner_result(1)
    inner_result(2)

    wait_bytes(sg.at[pl.ds(0, NZ - 1)], sg_sem.at[1])
    sg_copy = pltpu.make_async_copy(sg, sg_res, out_sem.at[2 * NI])
    sg_copy.start()
    inner_result(3)

    sg_copy.wait()
    for t in range(NI):
        ig_copy(t).wait()
        ag_copy(t).wait()

    for t in range(NI):
        cols = slice(OFFS[ORDER[t]], OFFS[ORDER[t]] + 128 * (ORDER[t] + 1))
        wait_bytes(cot_s.at[t, pl.ds(0, PD - 1)], c_ss.at[t])
        wait_bytes(g_s.at[t, pl.ds(0, PD - 1)], g_ss.at[t])
        @pl.when(h == 1)
        def _():
            cross(t, 0).wait_send()

        for part in range(1, PARTS):
            cross(t, part).wait_send()
        wait_bytes(rs_s.at[pl.ds(0, 7), :, cols], rs_ss.at[t])
        wait_bytes(ag.at[pl.ds(0, 7), :, cols], ag_ss.at[t])

        @pl.when(y != t)
        def _():
            wait_bytes(sy_s.at[t], sy_ss.at[t])

    for a in range(7):
        wait_bytes(ot, o_ss.at[a])
    wait_bytes(x_s.at[pl.ds(0, PD - 1)], x_sem.at[0])
    wait_bytes(ss_s.at[pl.ds(0, 7)], ss_sem.at[0])
    wait_bytes(sg.at[pl.ds(0, NZ - 1)], sg_sem.at[0])


def results_kernel(
    ig_in, ag_in, sg_in, ig_out, inner_out, outer_out, ig, ag, sg, inner, spread, outer, sem
):
    h = coords()[2]
    scale = 1.0 / math.sqrt(8192.0)
    load_ag = pltpu.make_async_copy(ag_in, ag, sem.at[1])
    load_ag.start()
    load_sg = pltpu.make_async_copy(sg_in, sg, sem.at[2])
    load_sg.start()
    load_ig = pltpu.make_async_copy(ig_in, ig, sem.at[0])
    load_ig.start()

    load_ag.wait()
    stores = []
    for k in range(NI):
        w = 128 * (k + 1)
        v = ag[:, :, OFFS[k]:OFFS[k] + w].astype(F32)
        for hh in range(2):
            start = k * 128 + hh * 64
            part = v[:, 8 * hh:8 * hh + 8, :].reshape(64, w) * scale
            keep = iota((64, w), 0) + start >= iota((64, w), 1)
            inner[start:start + 64, :w] = jnp.where(keep, part, 0.0)
            if w < B:
                inner[start:start + 64, w:] = jnp.zeros((64, B - w), F32)
        rows = pl.ds(k * 128, 128)
        stores.append(pltpu.make_async_copy(inner.at[rows], inner_out.at[rows], sem.at[3 + k]))
        stores[-1].start()

    load_ig.wait()
    whole = pltpu.make_async_copy(ig, ig_out, sem.at[4 + NI])
    whole.start()
    load_sg.wait()
    parts = []
    for hs in range(2):
        v = sg[hs * 8:(hs + 1) * 8].astype(F32).reshape(16, 16, 128)
        v = jnp.where(h == 0, v[:, :8], v[:, 8:])
        parts.append(v.reshape(128, 128).astype(BF))
    c_r = iota((128, 128), 0)
    c_c = iota((128, 128), 1)
    for bh in range(4):
        v = jnp.zeros((128, 128), F32)
        for hs in range(2):
            el = c_r - 32 * bh
            col = (el >= 0) & (el < 32) & (c_c == 16 * (el // 8) + 8 * hs + lax.rem(el, 8))
            v = v + dot_nn(parts[hs], col.astype(BF))
        for g in range(2):
            base = 32 * (bh % 2) + 16 * g + 8 * (bh // 2)
            keep = iota((64, 128), 0) // 8 + base >= iota((64, 128), 1)
            spread[base * 8:base * 8 + 64] = jnp.where(keep, v[64 * g:64 * g + 64] * scale, 0.0)
    for t in range(8):
        outer[t] = spread[pl.ds(t, 64, stride=8), :][:, :64]
    last = pltpu.make_async_copy(outer, outer_out, sem.at[3 + NI])
    last.start()
    whole.wait()
    for store in stores:
        store.wait()
    last.wait()


def local(activations, cotangent, inner_weight, outer_weight):
    vmem = pl.BlockSpec(memory_space=pltpu.VMEM)
    dma = pltpu.SemaphoreType.DMA
    scratch = [
        pltpu.VMEM((B, D), BF),
        pltpu.VMEM((B, D), BF),
        pltpu.VMEM((B, B), BF),
        pltpu.VMEM((8, 64, 64), BF),
        pltpu.VMEM((NI, PD, PP, CW), BF),
        pltpu.VMEM((NI, 2 * PD, PP, CW), BF),
        pltpu.VMEM((NI, PD, PP, CW), BF),
        pltpu.VMEM((NI, PD, PP, CW), BF),
        pltpu.VMEM((PD, NI, PP, CW), BF),
        pltpu.VMEM((PD, NI, PP, CW), BF),
        pltpu.VMEM((B, B), BF),
        pltpu.VMEM((B, B), BF),
        pltpu.VMEM((256, 128), F32),
        pltpu.VMEM((256, 128), BF),
        pltpu.VMEM((NI, 2, 256, 128), BF),
        pltpu.VMEM((NI, 512, 1024), BF),
        pltpu.VMEM((B, D), BF),
        pltpu.VMEM((B, D), F32),
        pltpu.VMEM((8, 16, PACK), BF),
        pltpu.VMEM((8, 16, PACK), BF),
        pltpu.VMEM((8, 16, PACK), BF),
        pltpu.VMEM((NI, 256, 128), BF),
        pltpu.VMEM((NI, 256, 128), BF),
        pltpu.VMEM((8, 32, 128), BF),
        pltpu.VMEM((8, 32, 128), BF),
        pltpu.VMEM((NZ, 32, 128), BF),
        dma((4,)),
        dma((NI,)), dma((NI,)),
        dma((NI, PARTS)), dma((NI, PARTS)),
        dma((2,)),
        dma((NI,)), dma((NI,)),
        dma((7,)), dma((8,)),
        dma((NI,)), dma((NI,)), dma((NI,)), dma((NI,)),
        dma((NI,)), dma((NI,)),
        dma((2,)), dma((2,)),
        dma((2 * NI + 1,)),
    ]
    hbm = pl.BlockSpec(memory_space=pltpu.HBM)
    sums = pl.pallas_call(
        kernel,
        out_shape=(
            jax.ShapeDtypeStruct((B, D), BF),
            jax.ShapeDtypeStruct((8, 16, PACK), BF),
            jax.ShapeDtypeStruct((NZ, 32, 128), BF),
        ),
        in_specs=[hbm] * 4,
        out_specs=(hbm, hbm, hbm),
        scratch_shapes=scratch,
        compiler_params=pltpu.CompilerParams(
            collective_id=0, has_side_effects=True, vmem_limit_bytes=62 * 1024 * 1024
        ),
        cost_estimate=pl.CostEstimate(flops=8_000_000_000, bytes_accessed=6_000_000, transcendentals=0),
        name="mixer",
    )(activations[0, 0], cotangent[0, 0], inner_weight[0], outer_weight)
    ig, inner_grad, outer_grad = pl.pallas_call(
        results_kernel,
        out_shape=(
            jax.ShapeDtypeStruct((B, D), BF),
            jax.ShapeDtypeStruct((B, B), F32),
            jax.ShapeDtypeStruct((8, 64, 64), F32),
        ),
        in_specs=[hbm] * 3,
        out_specs=(hbm, hbm, hbm),
        scratch_shapes=[
            pltpu.VMEM((B, D), BF),
            pltpu.VMEM((8, 16, PACK), BF),
            pltpu.VMEM((NZ, 32, 128), BF),
            pltpu.VMEM((B, B), F32),
            pltpu.VMEM((512, 128), F32),
            pltpu.VMEM((8, 64, 64), F32),
            dma((5 + NI,)),
        ],
        compiler_params=pltpu.CompilerParams(vmem_limit_bytes=62 * 1024 * 1024),
        cost_estimate=pl.CostEstimate(flops=50_000_000, bytes_accessed=5_000_000, transcendentals=0),
        name="results",
    )(*sums)
    return ig[None, None], inner_grad[None], outer_grad


def solution(mesh):
    placed = (
        P("dp", "seq", None, None),
        P("dp", "seq", None, None),
        P("seq", None, None),
        P("seq", None, None),
    )
    return jax.shard_map(
        local,
        mesh=mesh,
        in_specs=placed,
        out_specs=(P("dp", "seq", None, None), P("seq", None, None), P("seq", None, None)),
        check_vma=False,
    )
```

time: 345 us -> 156 us (0.45); the launches traced: 339 us -> 156 us
  waiting for transfers between devices: 227 us -> 0 us
  Pallas kernels: 0 us -> 155 us
  starting transfers between devices: 42.1 us -> 0 us
  local copies, waits for them, and re-layouts: 29.5 us -> 0 us
  other arithmetic: 17.9 us -> 0 us
  between operations: 14.2 us -> 0.64 us
  matrix products: 9 us -> 0 us
    psum x1 -> x0, waiting for transfers between devices: 157 us -> none  [local(): inner_sum, outer_sum = lax.psum((inner_sum, outer_sum), 'dp')]
    pallas_call x0 -> x2, Pallas kernels: none -> 155 us  [the longest x1 153 us: local(): pl.pallas_call(kernel, out_shape=(jax.ShapeDtypeStruct((B, D), BF), jax.S...]
    all_to_all x3 -> x0, waiting for transfers between devices: 69.7 us -> none  [the longest x1 30.9 us: local(): lax.all_to_all(outer_cols, 'seq', split_axis=1, concat_axis=2, tiled=True)]
    all_to_all x3 -> x0, starting transfers between devices: 42 us -> none  [the longest x1 22.4 us: local(): lax.all_to_all(cotangent, 'seq', split_axis=2, concat_axis=1, tiled=True)]
    unnamed x24 -> x0, local copies, waits for them, and re-layouts: 26.3 us -> none
    unnamed x2 -> x0, other arithmetic: 15.5 us -> none
    dot_general x5 -> x0, matrix products: 9 us -> none  [the longest x1 2.94 us: local(): jnp.einsum('snic,snjc->nij', mixed_grad, activations, preferred_element_t...]
  transfers between devices with their start and end apart: 4 -> 0, of which waited for: 4 -> 0; matrix products, arithmetic and copies ran while one was open for 10% -> 0% of each run, Pallas kernels for 0% -> 0%
where the time goes in v2:
time: 156 us
  Pallas kernels  155 us (99%)
    pallas_call x1, Pallas kernels, local(): pl.pallas_call(kernel, out_shape=(jax.ShapeDtypeStruct((B, D), BF), jax.S...  153 us

profile of v2, /device:TPU:1, one launch (start us, length us, event | category | flops | bytes accessed | tf_op | source)
XLA Modules:
  0.0 155.9 jit_solution(8216584281142460173)
XLA Ops:
  0.6 152.7 %mixer.1 = (bf16[512,1024]{1,0:T(8,128)(2,1)}, bf16[8,16,1280]{2,1,0:T(8,128)(2,1)}, bf16[16,32,128]{2,1,0:T(8,128)(2,1)}) custom-call(bf16[512,1024]{1,0:T(8,128)(2,1)} %bitcast.5, bf16[512,1024]{1,0:T(8,128)(2,1)} %bitcast.6, bf16[512,512]{1,0:T(8,128)(2,1)} %bitcast.9, bf16[8,64,64]{2,1,0:T(8,128)(2,1)} %outer_in.1), custom_call_target="tpu_custom_call" | custom-call | flops 8000000000 | bytes 6000000 | tf_op jit(solution)/shard_map/mixer/pallas_call | solution.py:565
  153.3 2.5 %results.1 = (bf16[512,1024]{1,0:T(8,128)(2,1)}, f32[512,512]{1,0:T(8,128)}, f32[8,64,64]{2,1,0:T(8,128)}) custom-call(bf16[512,1024]{1,0:T(8,128)(2,1)} %get-tuple-element.9.ig_in, bf16[8,16,1280]{2,1,0:T(8,128)(2,1)} %get-tuple-element.10.ag_in, bf16[16,32,128]{2,1,0:T(8,128)(2,1)} %get-tuple-element.11.sg_in), custom_call_target="tpu_custom_call" | custom-call | flops 50000000 | bytes 5000000 | tf_op jit(solution)/shard_map/results/pallas_call | solution.py:581

commit v3 on v2

--- a/solution.py
+++ b/solution.py
@@ -21,6 +21,7 @@
 NZ = 16
 OFFS = (0, 128, 384, 768)
 ORDER = (3, 2, 1, 0)
+TWO = (0, 1)
 PARTS = 4
 PACK = 1280
 
@@ -96,8 +97,8 @@
 def kernel(
     act_in, cot_in, inner_in, outer_in, ig_res, ag_res, sg_res,
     act, cot, inner, outer, cot_s, blk, g_s, g_r, x_s, x_r, inner_p, inner_t,
-    oscr, ot, ow, wmat, ig_out, ig_acc, rs_s, rs_r, ag, sy_s, sy_r, ss_s, ss_r, sg,
-    in_sem, c_ss, c_rs, z_ss, z_rs, x_sem, g_ss, g_rs, o_ss, o_rs, rs_ss, rs_rs, ag_ss, ag_rs,
+    oscr, ot, ow, wmat, ig_out, ig_acc, rs_s, rs_r, ag, sy_s, sy_r, ss_s, ss_r, sh, sg,
+    in_sem, c_ss, c_rs, z_ss, z_rs, x_sem, g_ss, g_rs, o_ss, o_rs, rs_ss, rs_rs, ag_ss, ag_rs, agp_rs, agf_rs,
     sy_ss, sy_rs, ss_sem, sg_sem, out_sem,
 ):
     lo, y, h, x, core = coords()
@@ -170,14 +171,6 @@
         rows = blk.at[ORDER[t], pl.ds(mine + part * size, size)]
         return remote(rows, rows, z_ss.at[t, part], z_rs.at[t, part], ring_peer(8)[1])
 
-    def cross_start(t):
-        @pl.when(h == 1)
-        def _():
-            cross(t, 0).start()
-
-        for part in range(1, PARTS):
-            cross(t, part).start()
-
     def cross_wait(t):
         size = PD // PARTS
         @pl.when(h == 0)
@@ -189,24 +182,31 @@
 
     def own_start(t):
         k = ORDER[t]
-        a2a_start(lambda d: cot_s.at[k, d], lambda d: blk.at[k, mine + d], c_ss.at[t], c_rs.at[t])
-
-    def own_wait(t):
-        wait_bytes(blk.at[ORDER[t], pl.ds(mine, PD)], c_rs.at[t])
-
-    for t in range(NI):
-        own_start(t)
-        if t == 0:
-            for a in range(1, 4):
-                remote(ot, ow.at[y, h], o_ss.at[a], o_rs.at[a], column_peer(a)[1]).start()
-            remote(ot, ow.at[y, h], o_ss.at[0], o_rs.at[0], ring_peer(8)[1]).start()
-            own_copy = pltpu.make_async_copy(ot, ow.at[y, h], o_rs.at[7])
-            own_copy.start()
-        if t > 0:
-            own_wait(t - 1)
-            cross_start(t - 1)
-    own_wait(NI - 1)
-    cross_start(NI - 1)
+        a2a_start(lambda d: cot_s.at[k, d], lambda d: blk.at[k, mine + d], c_ss.at[t], c_rs.at[t, y])
+
+    def cross_when_here(t):
+        size = PD // PARTS
+        for a in range(PARTS):
+            part = lax.rem(y + PARTS - a, PARTS)
+            wait_bytes(blk.at[ORDER[t], pl.ds(mine + part * size, size)], c_rs.at[t, part])
+
+            @pl.when(jnp.logical_or(h == 1, part > 0))
+            def _():
+                cross(t, part).start()
+
+    own_start(0)
+    for a in range(1, 4):
+        remote(ot, ow.at[y, h], o_ss.at[a], o_rs.at[a], column_peer(a)[1]).start()
+    remote(ot, ow.at[y, h], o_ss.at[0], o_rs.at[0], ring_peer(8)[1]).start()
+    own_copy = pltpu.make_async_copy(ot, ow.at[y, h], o_rs.at[7])
+    own_copy.start()
+    cross_when_here(0)
+    own_start(1)
+    own_start(2)
+    cross_when_here(1)
+    own_start(3)
+    cross_when_here(2)
+    cross_when_here(3)
 
     loads[2].wait()
 
@@ -357,10 +357,28 @@
             total = total + rs_r[i, :, cols].astype(F32)
         ag[lo, :, cols] = total.astype(BF)
 
+        if t in TWO:
+            for i in range(4):
+                own = ag.at[lo, :, cols]
+                device = half_peer(i)[1] if i else dp_peer(4)[1]
+                remote(own, own, ag_ss.at[t], ag_rs.at[t] if i else agp_rs.at[t], device).start()
+            return
+
         @pl.loop(1, 8)
         def _(i):
             remote(ag.at[lo, :, cols], ag.at[lo, :, cols], ag_ss.at[t], ag_rs.at[t], dp_peer(i)[1]).start()
 
+    def half_peer(i):
+        to = (lo // 4) * 4 + lax.rem(lo + i, 4)
+        return to, (to, y * 16 + h * 8 + x * 2 + core)
+
+    def forward(t):
+        cols = slice(OFFS[ORDER[t]], OFFS[ORDER[t]] + 128 * (ORDER[t] + 1))
+        theirs = ag.at[dp_peer(4)[0], :, cols]
+        wait_bytes(theirs, agp_rs.at[t])
+        for i in range(1, 4):
+            remote(theirs, theirs, ag_ss.at[t], agf_rs.at[t], half_peer(i)[1]).start()
+
     def ig_copy(t):
         rows = pl.ds(ORDER[t] * 128, 128)
         return pltpu.make_async_copy(ig_out.at[rows], ig_res.at[rows], out_sem.at[t])
@@ -371,7 +389,11 @@
 
     def inner_result(t):
         cols = slice(OFFS[ORDER[t]], OFFS[ORDER[t]] + 128 * (ORDER[t] + 1))
-        wait_bytes(ag.at[pl.ds(0, 7), :, cols], ag_rs.at[t])
+        if t in TWO:
+            wait_bytes(ag.at[pl.ds(0, 3), :, cols], ag_rs.at[t])
+            wait_bytes(ag.at[pl.ds(0, 3), :, cols], agf_rs.at[t])
+        else:
+            wait_bytes(ag.at[pl.ds(0, 7), :, cols], ag_rs.at[t])
         ag_copy(t).start()
 
     @pl.when(h == 1)
@@ -393,6 +415,7 @@
 
     mix(3)
     outer_part(3)
+    forward(0)
     back(3)
 
     for a in range(4):
@@ -413,16 +436,20 @@
     back_input(3)
     inner_result(0)
     gather(3)
+    forward(1)
 
     wait_bytes(ss_r, ss_sem.at[1])
     total = ss_r[0].astype(F32)
     for i in range(1, 8):
         total = total + ss_r[i].astype(F32)
-    sg[zme] = total.astype(BF)
+    for hh in range(2):
+        sh[hh] = jnp.concatenate([total[8 * hh:8 * hh + 8], total[16 + 8 * hh:24 + 8 * hh]], axis=0).astype(BF)
+    sg[zme] = sh[h]
 
     @pl.loop(1, NZ)
     def _(i):
-        remote(sg.at[zme], sg.at[zme], sg_sem.at[0], sg_sem.at[1], ring_peer(i)[1]).start()
+        z, device = ring_peer(i)
+        remote(sh.at[z // 8], sg.at[zme], sg_sem.at[0], sg_sem.at[1], device).start()
 
     inner_result(1)
     inner_result(2)
@@ -464,14 +491,17 @@
 def results_kernel(
     ig_in, ag_in, sg_in, ig_out, inner_out, outer_out, ig, ag, sg, inner, spread, outer, sem
 ):
-    h = coords()[2]
     scale = 1.0 / math.sqrt(8192.0)
     load_ag = pltpu.make_async_copy(ag_in, ag, sem.at[1])
     load_ag.start()
     load_sg = pltpu.make_async_copy(sg_in, sg, sem.at[2])
     load_sg.start()
-    load_ig = pltpu.make_async_copy(ig_in, ig, sem.at[0])
-    load_ig.start()
+    loads, wholes = [], []
+    for k in range(NI):
+        rows = pl.ds(k * 128, 128)
+        loads.append(pltpu.make_async_copy(ig_in.at[rows], ig.at[rows], sem.at[4 + NI + k]))
+        wholes.append(pltpu.make_async_copy(ig.at[rows], ig_out.at[rows], sem.at[4 + 2 * NI + k]))
+        loads[-1].start()
 
     load_ag.wait()
     stores = []
@@ -488,16 +518,13 @@
         rows = pl.ds(k * 128, 128)
         stores.append(pltpu.make_async_copy(inner.at[rows], inner_out.at[rows], sem.at[3 + k]))
         stores[-1].start()
-
-    load_ig.wait()
-    whole = pltpu.make_async_copy(ig, ig_out, sem.at[4 + NI])
-    whole.start()
+        loads[k].wait()
+        wholes[k].start()
+
     load_sg.wait()
     parts = []
     for hs in range(2):
-        v = sg[hs * 8:(hs + 1) * 8].astype(F32).reshape(16, 16, 128)
-        v = jnp.where(h == 0, v[:, :8], v[:, 8:])
-        parts.append(v.reshape(128, 128).astype(BF))
+        parts.append(sg[hs * 8:(hs + 1) * 8].reshape(128, 128))
     c_r = iota((128, 128), 0)
     c_c = iota((128, 128), 1)
     for bh in range(4):
@@ -514,8 +541,7 @@
         outer[t] = spread[pl.ds(t, 64, stride=8), :][:, :64]
     last = pltpu.make_async_copy(outer, outer_out, sem.at[3 + NI])
     last.start()
-    whole.wait()
-    for store in stores:
+    for store in stores + wholes:
         store.wait()
     last.wait()
 
@@ -549,14 +575,15 @@
         pltpu.VMEM((NI, 256, 128), BF),
         pltpu.VMEM((8, 32, 128), BF),
         pltpu.VMEM((8, 32, 128), BF),
-        pltpu.VMEM((NZ, 32, 128), BF),
+        pltpu.VMEM((2, 16, 128), BF),
+        pltpu.VMEM((NZ, 16, 128), BF),
         dma((4,)),
-        dma((NI,)), dma((NI,)),
+        dma((NI,)), dma((NI, PARTS)),
         dma((NI, PARTS)), dma((NI, PARTS)),
         dma((2,)),
         dma((NI,)), dma((NI,)),
         dma((7,)), dma((8,)),
-        dma((NI,)), dma((NI,)), dma((NI,)), dma((NI,)),
+        dma((NI,)), dma((NI,)), dma((NI,)), dma((NI,)), dma((NI,)), dma((NI,)),
         dma((NI,)), dma((NI,)),
         dma((2,)), dma((2,)),
         dma((2 * NI + 1,)),
@@ -567,7 +594,7 @@
         out_shape=(
             jax.ShapeDtypeStruct((B, D), BF),
             jax.ShapeDtypeStruct((8, 16, PACK), BF),
-            jax.ShapeDtypeStruct((NZ, 32, 128), BF),
+            jax.ShapeDtypeStruct((NZ, 16, 128), BF),
         ),
         in_specs=[hbm] * 4,
         out_specs=(hbm, hbm, hbm),
@@ -590,11 +617,11 @@
         scratch_shapes=[
             pltpu.VMEM((B, D), BF),
             pltpu.VMEM((8, 16, PACK), BF),
-            pltpu.VMEM((NZ, 32, 128), BF),
+            pltpu.VMEM((NZ, 16, 128), BF),
             pltpu.VMEM((B, B), F32),
             pltpu.VMEM((512, 128), F32),
             pltpu.VMEM((8, 64, 64), F32),
-            dma((5 + NI,)),
+            dma((4 + 3 * NI,)),
         ],
         compiler_params=pltpu.CompilerParams(vmem_limit_bytes=62 * 1024 * 1024),
         cost_estimate=pl.CostEstimate(flops=50_000_000, bytes_accessed=5_000_000, transcendentals=0),

time: 156 us -> 151 us (0.968)
  Pallas kernels: 155 us -> 150 us
    pallas_call x1, Pallas kernels: 153 us -> 147 us  [local(): pl.pallas_call(kernel, out_shape=(jax.ShapeDtypeStruct((B, D), BF), jax.S...]
where the time goes in v3:
time: 151 us; the launch traced here: 150 us
  Pallas kernels  150 us (99%)
    pallas_call x1, Pallas kernels, local(): pl.pallas_call(kernel, out_shape=(jax.ShapeDtypeStruct((B, D), BF), jax.S...  147 us

profile of v3, /device:TPU:1, one launch (start us, length us, event | category | flops | bytes accessed | tf_op | source)
XLA Modules:
  0.0 150.4 jit_solution(6644529332815139426)
XLA Ops:
  0.6 147.2 %mixer.1 = (bf16[512,1024]{1,0:T(8,128)(2,1)}, bf16[8,16,1280]{2,1,0:T(8,128)(2,1)}, bf16[16,16,128]{2,1,0:T(8,128)(2,1)}) custom-call(bf16[512,1024]{1,0:T(8,128)(2,1)} %bitcast.5, bf16[512,1024]{1,0:T(8,128)(2,1)} %bitcast.6, bf16[512,512]{1,0:T(8,128)(2,1)} %bitcast.9, bf16[8,64,64]{2,1,0:T(8,128)(2,1)} %outer_in.1), custom_call_target="tpu_custom_call" | custom-call | flops 8000000000 | bytes 6000000 | tf_op jit(solution)/shard_map/mixer/pallas_call | solution.py:592
  147.8 2.5 %results.1 = (bf16[512,1024]{1,0:T(8,128)(2,1)}, f32[512,512]{1,0:T(8,128)}, f32[8,64,64]{2,1,0:T(8,128)}) custom-call(bf16[512,1024]{1,0:T(8,128)(2,1)} %get-tuple-element.9.ig_in, bf16[8,16,1280]{2,1,0:T(8,128)(2,1)} %get-tuple-element.10.ag_in, bf16[16,16,128]{2,1,0:T(8,128)(2,1)} %get-tuple-element.11.sg_in), custom_call_target="tpu_custom_call" | custom-call | flops 50000000 | bytes 5000000 | tf_op jit(solution)/shard_map/results/pallas_call | solution.py:608

commit v4 on v3

--- a/solution.py
+++ b/solution.py
@@ -97,8 +97,8 @@
 def kernel(
     act_in, cot_in, inner_in, outer_in, ig_res, ag_res, sg_res,
     act, cot, inner, outer, cot_s, blk, g_s, g_r, x_s, x_r, inner_p, inner_t,
-    oscr, ot, ow, wmat, ig_out, ig_acc, rs_s, rs_r, ag, sy_s, sy_r, ss_s, ss_r, sh, sg,
-    in_sem, c_ss, c_rs, z_ss, z_rs, x_sem, g_ss, g_rs, o_ss, o_rs, rs_ss, rs_rs, ag_ss, ag_rs, agp_rs, agf_rs,
+    oscr, ot, ow, wmat, g_own, s_own, ig_out, ig_acc, rs_s, rs_r, ex_m, ex_s, ex_r, ag, sy_s, sy_r, ss_s, ss_r, sh, sg,
+    in_sem, c_ss, c_rs, z_ss, z_rs, x_sem, g_ss, g_rs, o_ss, o_rs, rs_ss, rs_rs, ag_ss, ag_rs, agp_rs, agf_rs, ex_ss, ex_rs,
     sy_ss, sy_rs, ss_sem, sg_sem, out_sem,
 ):
     lo, y, h, x, core = coords()
@@ -154,11 +154,19 @@
             cot_s[big, quarter * 8 + u * 2 + 1] = second[:, cols]
 
     loads[1].wait()
-    low = iota((64, 64), 0) >= iota((64, 64), 1)
-    for t in range(8):
-        v = jnp.where(low, outer[t].astype(F32), 0.0)
-        oscr[pl.ds(t, 32, stride=8), :] = jnp.concatenate([v[:32], v[32:]], axis=1)
-    ot[...] = oscr[...].astype(BF)
+    keep = iota((8, 64, 64), 1) >= iota((8, 64, 64), 2)
+    factors = jnp.where(keep, outer[...].astype(F32), 0.0).astype(BF)
+    lane = iota((64, 128), 1)
+    el = lax.rem(lane, 32)
+    for side in range(2):
+        total = jnp.zeros((128, 128), F32)
+        for q in range(4):
+            block = 16 * (el // 8) + 8 * side + lax.rem(el, 8)
+            sel = ((iota((64, 128), 0) == block) & (lane // 32 == q)).astype(BF)
+            total = total + dot_nn(factors[:, 16 * q:16 * q + 16].reshape(128, 64), sel)
+        for t in range(8):
+            oscr[pl.ds(t, 16, stride=8), :] = total[16 * t:16 * t + 16]
+        ot[side] = oscr[...].astype(BF)
 
     pl.semaphore_wait(barrier, PD - 1 + NZ - 1)
 
@@ -196,9 +204,9 @@
 
     own_start(0)
     for a in range(1, 4):
-        remote(ot, ow.at[y, h], o_ss.at[a], o_rs.at[a], column_peer(a)[1]).start()
-    remote(ot, ow.at[y, h], o_ss.at[0], o_rs.at[0], ring_peer(8)[1]).start()
-    own_copy = pltpu.make_async_copy(ot, ow.at[y, h], o_rs.at[7])
+        remote(ot.at[h], ow.at[y, h], o_ss.at[a], o_rs.at[a], column_peer(a)[1]).start()
+    remote(ot.at[1 - h], ow.at[y, h], o_ss.at[0], o_rs.at[0], ring_peer(8)[1]).start()
+    own_copy = pltpu.make_async_copy(ot.at[h], ow.at[y, h], o_rs.at[7])
     own_copy.start()
     cross_when_here(0)
     own_start(1)
@@ -250,21 +258,45 @@
             wait_bytes(ow.at[src, 1 - h], o_rs.at[3 + a])
 
     def build(k):
-        el = iota((64, 512), 1) // 16
-        pick = (iota((64, 512), 0) == 16 * (el // 8) + 8 * h + lax.rem(el, 8)).astype(BF)
-        same = lax.rem(iota((128, 512), 0), 16) == lax.rem(iota((128, 512), 1), 16)
+        lane = iota((128, 512), 0)
+        el = iota((128, 512), 1) // 16
+        same = lax.rem(lane, 16) == lax.rem(iota((128, 512), 1), 16)
 
         @pl.loop(0, 8)
         def _(g):
             group = 2 * lax.rem(g, 4) + g // 4
-            rows = pl.ds(pl.multiple_of(lax.rem(group, 4) * 64, 64), 64)
-            both = []
-            for hh in range(2):
-                v = ow[k, hh, rows, :].astype(F32)
-                both.append(jnp.where(group < 4, v[:, :64], v[:, 64:]).reshape(8, 8, 64))
-            v = jnp.concatenate(both, axis=1).reshape(128, 64).astype(BF)
-            w = jnp.where(same, dot_nn(v, pick), 0.0).astype(BF)
-            wmat[k, :, pl.ds(pl.multiple_of(g * 128, 128), 128)] = w.T
+            rows = pl.ds(pl.multiple_of(lax.rem(group, 2) * 64, 64), 64)
+            put = (lane == 32 * (group // 2) + el).astype(BF)
+            both = [dot_nn(ow[k, hh, rows, :], put).reshape(8, 8, 512) for hh in range(2)]
+            w = jnp.concatenate(both, axis=1).reshape(128, 512)
+            wmat[k, :, pl.ds(pl.multiple_of(g * 128, 128), 128)] = jnp.where(same, w, 0.0).astype(BF).T
+
+    theirs = pl.ds(pl.multiple_of((1 - h) * 512, 512), 512)
+
+    def quarters(t, half, side):
+        k = ORDER[t]
+        same = lax.rem(iota((128, 512), 0), 16) == lax.rem(iota((128, 512), 1), 16)
+        total = jnp.zeros((128, 128), F32)
+        for i in range(2):
+            bh = 2 * side + i
+            v = dot_nt(blk[k, pl.ds(bh * 16 + half * 8, 8)].reshape(128, CW), x_r[:, k].reshape(512, CW))
+            put = (iota((512, 128), 1) == 32 * bh + iota((512, 128), 0) // 16).astype(BF)
+            total = total + dot_nn(jnp.where(same, v, 0.0).astype(BF), put)
+        return total
+
+    def own_products():
+        t = NI - 1
+        k = ORDER[t]
+        ours = pl.ds(pl.multiple_of(h * 512, 512), 512)
+
+        @pl.loop(0, 4)
+        def _(q):
+            rows = pl.ds(pl.multiple_of(q * 128, 128), 128)
+            g_own[rows, :] = dot_nn(wmat[k, rows, ours], blk[k, pl.ds(mine, PD)].reshape(512, CW))
+
+        @pl.loop(0, 2)
+        def _(half):
+            s_own[pl.ds(pl.multiple_of(half * 128, 128), 128), :] = quarters(t, half, h)
 
     def mix(t):
         k = ORDER[t]
@@ -274,7 +306,11 @@
         def _(a):
             place, seq = peer_row(a)
             rows = pl.ds(pl.multiple_of(place * PP, 128), 128)
-            v = dot_nn(wmat[k, rows, :], blk[k].reshape(1024, CW)).astype(BF)
+            if t == NI - 1:
+                v = dot_nn(wmat[k, rows, theirs], blk[k, pl.ds(other, PD)].reshape(512, CW))
+                v = (v + g_own[rows, :]).astype(BF)
+            else:
+                v = dot_nn(wmat[k, rows, :], blk[k].reshape(1024, CW)).astype(BF)
             g_s[k, pl.ds(place, 8)] = v.reshape(8, PP, CW)
 
             def give(off):
@@ -295,16 +331,14 @@
         k = ORDER[t]
         if t == 0:
             wait_bytes(x_r, x_sem.at[1])
-        same = lax.rem(iota((128, 512), 0), 16) == lax.rem(iota((128, 512), 1), 16)
-
         @pl.loop(0, 2)
         def _(half):
-            total = jnp.zeros((128, 128), F32)
-            for bh in range(4):
-                v = dot_nt(blk[k, pl.ds(bh * 16 + half * 8, 8)].reshape(128, CW), x_r[:, k].reshape(512, CW))
-                put = (iota((512, 128), 1) == 32 * bh + iota((512, 128), 0) // 16).astype(BF)
-                total = total + dot_nn(jnp.where(same, v, 0.0).astype(BF), put)
-            sy_s[k, pl.ds(pl.multiple_of(half * 128, 128), 128), :] = total.astype(BF)
+            rows = pl.ds(pl.multiple_of(half * 128, 128), 128)
+            if t == NI - 1:
+                total = s_own[rows, :] + quarters(t, half, 1 - h)
+            else:
+                total = quarters(t, half, 0) + quarters(t, half, 1)
+            sy_s[k, rows, :] = total.astype(BF)
 
         @pl.when(y == k)
         def _():
@@ -326,12 +360,41 @@
         cols = slice(OFFS[k], OFFS[k] + w)
         rs_s[:, :, cols] = v.astype(BF).reshape(8, 16, w)
 
+        if t in TWO:
+            at = lax.rem(lo, 4)
+            for half in (0, 4):
+                for i in range(1, 4):
+                    to, device = half_peer(i)
+                    src = rs_s.at[lax.rem(to, 4) + half, :, cols]
+                    remote(src, rs_r.at[at + half, :, cols], rs_ss.at[t], rs_rs.at[t], device).start()
+                pltpu.make_async_copy(
+                    rs_s.at[at + half, :, cols], rs_r.at[at + half, :, cols], rs_rs.at[t]
+                ).start()
+            return
+
         @pl.loop(1, 8)
         def _(i):
             to, device = dp_peer(i)
             remote(rs_s.at[to, :, cols], rs_r.at[lo, :, cols], rs_ss.at[t], rs_rs.at[t], device).start()
 
         pltpu.make_async_copy(rs_s.at[lo, :, cols], rs_r.at[lo, :, cols], rs_rs.at[t]).start()
+
+    def exchange(t):
+        cols = slice(OFFS[ORDER[t]], OFFS[ORDER[t]] + 128 * (ORDER[t] + 1))
+        wait_bytes(rs_r.at[:, :, cols], rs_rs.at[t])
+        sums = []
+        for half in (0, 4):
+            total = rs_r[half, :, cols].astype(F32)
+            for i in range(1, 4):
+                total = total + rs_r[half + i, :, cols].astype(F32)
+            sums.append(total)
+        ex_m[:, cols] = jnp.where(lo < 4, sums[0], sums[1])
+        ex_s[:, cols] = jnp.where(lo < 4, sums[1], sums[0]).astype(BF)
+        remote(ex_s.at[:, cols], ex_r.at[:, cols], ex_ss.at[t], ex_rs.at[t], dp_peer(4)[1]).start()
+
+    def half_peer(i):
+        to = (lo // 4) * 4 + lax.rem(lo + i, 4)
+        return to, (to, y * 16 + h * 8 + x * 2 + core)
 
     def back_input(t):
         k = ORDER[t]
@@ -351,10 +414,14 @@
         k = ORDER[t]
         w = 128 * (k + 1)
         cols = slice(OFFS[k], OFFS[k] + w)
-        wait_bytes(rs_r.at[:, :, cols], rs_rs.at[t])
-        total = rs_r[0, :, cols].astype(F32)
-        for i in range(1, 8):
-            total = total + rs_r[i, :, cols].astype(F32)
+        if t in TWO:
+            wait_bytes(ex_r.at[:, cols], ex_rs.at[t])
+            total = ex_m[:, cols] + ex_r[:, cols].astype(F32)
+        else:
+            wait_bytes(rs_r.at[:, :, cols], rs_rs.at[t])
+            total = rs_r[0, :, cols].astype(F32)
+            for i in range(1, 8):
+                total = total + rs_r[i, :, cols].astype(F32)
         ag[lo, :, cols] = total.astype(BF)
 
         if t in TWO:
@@ -367,10 +434,6 @@
         @pl.loop(1, 8)
         def _(i):
             remote(ag.at[lo, :, cols], ag.at[lo, :, cols], ag_ss.at[t], ag_rs.at[t], dp_peer(i)[1]).start()
-
-    def half_peer(i):
-        to = (lo // 4) * 4 + lax.rem(lo + i, 4)
-        return to, (to, y * 16 + h * 8 + x * 2 + core)
 
     def forward(t):
         cols = slice(OFFS[ORDER[t]], OFFS[ORDER[t]] + 128 * (ORDER[t] + 1))
@@ -411,11 +474,13 @@
         back(t)
         back_input(t)
         if t == 2:
-            gather(0)
-
+            exchange(0)
+
+    own_products()
     mix(3)
     outer_part(3)
-    forward(0)
+    gather(0)
+    exchange(1)
     back(3)
 
     for a in range(4):
@@ -434,8 +499,8 @@
     gather(1)
     gather(2)
     back_input(3)
-    inner_result(0)
     gather(3)
+    forward(0)
     forward(1)
 
     wait_bytes(ss_r, ss_sem.at[1])
@@ -451,6 +516,7 @@
         z, device = ring_peer(i)
         remote(sh.at[z // 8], sg.at[zme], sg_sem.at[0], sg_sem.at[1], device).start()
 
+    inner_result(0)
     inner_result(1)
     inner_result(2)
 
@@ -474,7 +540,11 @@
 
         for part in range(1, PARTS):
             cross(t, part).wait_send()
-        wait_bytes(rs_s.at[pl.ds(0, 7), :, cols], rs_ss.at[t])
+        if t in TWO:
+            wait_bytes(rs_s.at[pl.ds(0, 6), :, cols], rs_ss.at[t])
+            wait_bytes(ex_s.at[:, cols], ex_ss.at[t])
+        else:
+            wait_bytes(rs_s.at[pl.ds(0, 7), :, cols], rs_ss.at[t])
         wait_bytes(ag.at[pl.ds(0, 7), :, cols], ag_ss.at[t])
 
         @pl.when(y != t)
@@ -482,7 +552,7 @@
             wait_bytes(sy_s.at[t], sy_ss.at[t])
 
     for a in range(7):
-        wait_bytes(ot, o_ss.at[a])
+        wait_bytes(ot.at[0], o_ss.at[a])
     wait_bytes(x_s.at[pl.ds(0, PD - 1)], x_sem.at[0])
     wait_bytes(ss_s.at[pl.ds(0, 7)], ss_sem.at[0])
     wait_bytes(sg.at[pl.ds(0, NZ - 1)], sg_sem.at[0])
@@ -562,14 +632,19 @@
         pltpu.VMEM((PD, NI, PP, CW), BF),
         pltpu.VMEM((B, B), BF),
         pltpu.VMEM((B, B), BF),
+        pltpu.VMEM((128, 128), F32),
+        pltpu.VMEM((2, 128, 128), BF),
+        pltpu.VMEM((NI, 2, 128, 128), BF),
+        pltpu.VMEM((NI, 512, 1024), BF),
+        pltpu.VMEM((512, CW), F32),
         pltpu.VMEM((256, 128), F32),
-        pltpu.VMEM((256, 128), BF),
-        pltpu.VMEM((NI, 2, 256, 128), BF),
-        pltpu.VMEM((NI, 512, 1024), BF),
         pltpu.VMEM((B, D), BF),
         pltpu.VMEM((B, D), F32),
         pltpu.VMEM((8, 16, PACK), BF),
         pltpu.VMEM((8, 16, PACK), BF),
+        pltpu.VMEM((16, PACK), F32),
+        pltpu.VMEM((16, PACK), BF),
+        pltpu.VMEM((16, PACK), BF),
         pltpu.VMEM((8, 16, PACK), BF),
         pltpu.VMEM((NI, 256, 128), BF),
         pltpu.VMEM((NI, 256, 128), BF),
@@ -584,6 +659,7 @@
         dma((NI,)), dma((NI,)),
         dma((7,)), dma((8,)),
         dma((NI,)), dma((NI,)), dma((NI,)), dma((NI,)), dma((NI,)), dma((NI,)),
+        dma((NI,)), dma((NI,)),
         dma((NI,)), dma((NI,)),
         dma((2,)), dma((2,)),
         dma((2 * NI + 1,)),

time: 151 us -> 147 us (0.974)
  Pallas kernels: 150 us -> 146 us
    pallas_call x1, Pallas kernels: 147 us -> 144 us  [local(): pl.pallas_call(kernel, out_shape=(jax.ShapeDtypeStruct((B, D), BF), jax.S...]
where the time goes in v4:
time: 147 us
  Pallas kernels  146 us (99%)
    pallas_call x1, Pallas kernels, local(): pl.pallas_call(kernel, out_shape=(jax.ShapeDtypeStruct((B, D), BF), jax.S...  144 us

profile of v4, /device:TPU:1, one launch (start us, length us, event | category | flops | bytes accessed | tf_op | source)
XLA Modules:
  0.0 146.7 jit_solution(15461868530369648613)
XLA Ops:
  0.6 143.5 %mixer.1 = (bf16[512,1024]{1,0:T(8,128)(2,1)}, bf16[8,16,1280]{2,1,0:T(8,128)(2,1)}, bf16[16,16,128]{2,1,0:T(8,128)(2,1)}) custom-call(bf16[512,1024]{1,0:T(8,128)(2,1)} %bitcast.5, bf16[512,1024]{1,0:T(8,128)(2,1)} %bitcast.6, bf16[512,512]{1,0:T(8,128)(2,1)} %bitcast.9, bf16[8,64,64]{2,1,0:T(8,128)(2,1)} %outer_in.1), custom_call_target="tpu_custom_call" | custom-call | flops 8000000000 | bytes 6000000 | tf_op jit(solution)/shard_map/mixer/pallas_call | solution.py:668
  144.2 2.5 %results.1 = (bf16[512,1024]{1,0:T(8,128)(2,1)}, f32[512,512]{1,0:T(8,128)}, f32[8,64,64]{2,1,0:T(8,128)}) custom-call(bf16[512,1024]{1,0:T(8,128)(2,1)} %get-tuple-element.9.ig_in, bf16[8,16,1280]{2,1,0:T(8,128)(2,1)} %get-tuple-element.10.ag_in, bf16[16,16,128]{2,1,0:T(8,128)(2,1)} %get-tuple-element.11.sg_in), custom_call_target="tpu_custom_call" | custom-call | flops 50000000 | bytes 5000000 | tf_op jit(solution)/shard_map/results/pallas_call | solution.py:684

commit v5 on v4

--- a/solution.py
+++ b/solution.py
@@ -501,7 +501,6 @@
     back_input(3)
     gather(3)
     forward(0)
-    forward(1)
 
     wait_bytes(ss_r, ss_sem.at[1])
     total = ss_r[0].astype(F32)
@@ -516,6 +515,7 @@
         z, device = ring_peer(i)
         remote(sh.at[z // 8], sg.at[zme], sg_sem.at[0], sg_sem.at[1], device).start()
 
+    forward(1)
     inner_result(0)
     inner_result(1)
     inner_result(2)

time: 147 us -> 146 us (level)
  no operation moved by 1% of the time
where the time goes in v5:
time: 146 us
  Pallas kernels  145 us (99%)
    pallas_call x1, Pallas kernels, local(): pl.pallas_call(kernel, out_shape=(jax.ShapeDtypeStruct((B, D), BF), jax.S...  143 us

profile of v5, /device:TPU:1, one launch (start us, length us, event | category | flops | bytes accessed | tf_op | source)
XLA Modules:
  0.0 145.9 jit_solution(9172923051560533726)
XLA Ops:
  0.6 142.8 %mixer.1 = (bf16[512,1024]{1,0:T(8,128)(2,1)}, bf16[8,16,1280]{2,1,0:T(8,128)(2,1)}, bf16[16,16,128]{2,1,0:T(8,128)(2,1)}) custom-call(bf16[512,1024]{1,0:T(8,128)(2,1)} %bitcast.5, bf16[512,1024]{1,0:T(8,128)(2,1)} %bitcast.6, bf16[512,512]{1,0:T(8,128)(2,1)} %bitcast.9, bf16[8,64,64]{2,1,0:T(8,128)(2,1)} %outer_in.1), custom_call_target="tpu_custom_call" | custom-call | flops 8000000000 | bytes 6000000 | tf_op jit(solution)/shard_map/mixer/pallas_call | solution.py:668
  143.4 2.5 %results.1 = (bf16[512,1024]{1,0:T(8,128)(2,1)}, f32[512,512]{1,0:T(8,128)}, f32[8,64,64]{2,1,0:T(8,128)}) custom-call(bf16[512,1024]{1,0:T(8,128)(2,1)} %get-tuple-element.9.ig_in, bf16[8,16,1280]{2,1,0:T(8,128)(2,1)} %get-tuple-element.10.ag_in, bf16[16,16,128]{2,1,0:T(8,128)(2,1)} %get-tuple-element.11.sg_in), custom_call_target="tpu_custom_call" | custom-call | flops 50000000 | bytes 5000000 | tf_op jit(solution)/shard_map/results/pallas_call | solution.py:684
